TPU v7x, 256 devices: a whole 4x4x8 slice. The times are simulated.
256 devices in a mesh: tile: 32 (over z, y), lev: 8 (over x, core).
Axes of the slice: x: 4, y: 4, z: 8, core: 2. Of those that a mesh axis runs over, the one named last changes fastest.
Arguments:
- members: bfloat16 [32, 65536, 128], P('lev', 'tile'), may hold values from -4 to 4
- obs_operator: bfloat16 [8, 2048, 4, 128, 128], P('lev', 'tile'), as said below
- col_level: int32 [8, 2048, 4], P('lev', 'tile'), may hold values from 0 to 3
- col_block: int32 [8, 2048, 4], P('lev', 'tile'), may hold values from 0 to 19, as said below
- obs_count: int32 [2048], P(('tile', 'lev')), may hold values from 1 to 128, as said below
- obs_values: float32 [2048, 128], P(('tile', 'lev')), may hold values from -60 to 60
- obs_weight: float32 [2048, 128], P(('tile', 'lev')), may hold values from 0.01 to 0.18
Outputs:
- analysed: bfloat16 [32, 65536, 128], P('lev', 'tile')
- transform: float32 [128, 128], replicated
Inputs may be any that keep to these rules, and one draw needn't show every extreme that they name: `col_block`: for the observation block in position i of its tile (i < 64), every column block lies within 2 of i * 16 // 64 + 2, and never names a block outside the grid. `obs_count`: the first block of every tile uses all 128 rows. `obs_operator`: entries lie within 4 / sqrt(8192) of zero.
All inputs are finite; a program needn't handle non-finite values.
Results may differ from a plain program's by a relative error of at most 0.0076.
Values may be sent and summed in bfloat16 or wider, within the bound.
No kernel may reach another device: no remote copies, remote signals or barrier semaphores. Data moves between devices by JAX's collectives and lax.ppermute only.
A program may use at most 128 MiB of HBM per device.

v0:
```python
import math
import jax
import jax.numpy as jnp
from jax import lax
from jax.sharding import PartitionSpec as P

HALO = 2


def with_halo(value, sides, width):
    for axis, dim in sides:
        count, length = (lax.axis_size(axis), value.shape[dim])
        up = [(i, (i + 1) % count) for i in range(count - 1)]
        down = [(j, i) for i, j in up]
        last = lax.slice_in_dim(value, length - width, length, axis=dim)
        first = lax.slice_in_dim(value, 0, width, axis=dim)
        before = lax.ppermute(last, axis, up)
        after = lax.ppermute(first, axis, down)
        value = jnp.concatenate([before, value, after], axis=dim)
    return value


def shards(members, obs_operator, col_level, col_block, obs_count, obs_values, obs_weight):
    highest = lax.Precision.HIGHEST
    lev_local, cells_local, ensemble = members.shape
    block_size = obs_operator.shape[-1]
    rim_cells = HALO * block_size
    padded = with_halo(members, (("tile", 1),), rim_cells)
    window_blocks = padded.shape[1] // block_size
    column_blocks = padded.reshape(lev_local, window_blocks, block_size, ensemble).reshape(
        lev_local * window_blocks, block_size, ensemble
    )
    operator_blocks = obs_operator[0]
    flat_index = col_level[0] * window_blocks + col_block[0]
    live_rows = (jnp.arange(block_size, dtype=jnp.int32)[None, :] < obs_count[:, None]).astype(
        jnp.float32
    )
    weight_local = obs_weight * live_rows
    chosen = column_blocks[flat_index]
    observed = lax.psum_scatter(
        jnp.einsum("okij,okjm->oim", operator_blocks, chosen, preferred_element_type=jnp.float32),
        "lev",
        scatter_dimension=0,
        tiled=True,
    )
    weight, values_used = (weight_local, obs_values)
    mean_obs = jnp.sum(observed, axis=2) / ensemble
    row_scale = weight / math.sqrt(ensemble - 1)
    spread = ((observed - mean_obs[:, :, None]) * row_scale[:, :, None]).reshape(-1, ensemble)
    innovation = ((values_used - mean_obs) * weight).reshape(-1)
    gram_local = jnp.dot(spread.T, spread, precision=highest, preferred_element_type=jnp.float32)
    pull_local = jnp.dot(innovation, spread, precision=highest, preferred_element_type=jnp.float32)
    identity = jnp.eye(ensemble, dtype=jnp.float32)
    gram, pull = lax.psum((gram_local, pull_local), ("tile", "lev"))
    lower = jnp.linalg.cholesky(identity + gram)
    inverse = lax.linalg.triangular_solve(lower, identity, left_side=True, lower=True)
    shift_weights = jnp.dot(inverse.T, jnp.dot(inverse, pull, precision=highest), precision=highest)
    transform = shift_weights[:, None] / math.sqrt(ensemble - 1) + inverse.T
    transform_bf = transform.astype(jnp.bfloat16)
    row_mean = jnp.sum(members, axis=2, dtype=jnp.float32) / ensemble
    anomalies = (members.astype(jnp.float32) - row_mean[:, :, None]).astype(jnp.bfloat16)
    moved = jnp.dot(
        anomalies.reshape(-1, ensemble), transform_bf, preferred_element_type=jnp.float32
    )
    analysed = (row_mean[:, :, None] + moved.reshape(lev_local, cells_local, ensemble)).astype(
        jnp.bfloat16
    )
    return (analysed, transform)


def solution(mesh):
    placed = (
        P("lev", "tile", None),
        P("lev", "tile", None, None, None),
        P("lev", "tile", None),
        P("lev", "tile", None),
        P(("tile", "lev")),
        P(("tile", "lev"), None),
        P(("tile", "lev"), None),
    )
    return jax.shard_map(
        shards, mesh=mesh, in_specs=placed, out_specs=(P("lev", "tile", None), P()), check_vma=False
    )
```

profile of v0, /device:TPU:1, one launch (start us, length us, event | category | flops | bytes accessed | tf_op | source)
XLA Modules:
  0.0 369.6 jit_solution(11171952963979726350)
XLA Ops:
  7.2 1.1 fusion.23
  8.3 4.0 %collective-permute-start = (bf16[4,256,128]{2,1,0:T(8,128)(2,1)S(1)}, bf16[4,256,128]{2,1,0:T(8,128)(2,1)S(1)}, u32[]{:S(2)}, u32[]{:S(2)}) collective-permute-start(bf16[4,256,128]{2,1,0:T(8,128)(2,1)S(1)} %get-tuple-element.6), channel_id=1, source_target_pairs={{0,8},{8,16},{16,24},{24,32},{32,40},{40,48},{48,56},{56,64},{64,7... | collective-permute-start | bytes 786440 | tf_op jit(solution)/shard_map/ppermute | solution.py:17
  12.3 1.3 collective-permute-start.1
  13.6 0.7 compare_select_fusion
  14.3 0.1 copy.14
  14.4 0.1 reshape.63
  14.6 2.7 collective-permute-done
  17.3 3.8 %collective-permute-done.1 = bf16[4,256,128]{2,1,0:T(8,128)(2,1)S(1)} collective-permute-done((bf16[4,256,128]{2,1,0:T(8,128)(2,1)S(1)}, bf16[4,256,128]{2,1,0:T(8,128)(2,1)S(1)}, u32[]{:S(2)}, u32[]{:S(2)}) %collective-permute-start.1) | collective-permute-done | bytes 262176 | tf_op jit(solution)/shard_map/ppermute | solution.py:18
  21.1 1.8 pad_maximum_fusion
  22.9 8.6 %gather_fusion = bf16[256,128,128]{2,1,0:T(8,128)(2,1)} fusion(bf16[80,128,128]{2,1,0:T(8,128)(2,1)S(1)} %bitcast.54, s32[1024]{0:T(1024)S(1)} %pad_clamp_fusion), kind=kCustom, calls=%fused_computation | custom fusion | bytes 16778240 | tf_op jit(solution)/shard_map/gather | solution.py:39
  31.5 10.1 %fusion.3 = f32[64,128,128]{1,2,0:T(8,128)} fusion(bf16[64,4,128,128]{3,2,1,0:T(8,128)(2,1)} %bitcast.55, bf16[1,64,4,128,128]{4,3,2,1,0:T(8,128)(2,1)} %param.8), kind=kOutput, calls=%fused_computation.8 | convolution fusion | flops 1073741824 | bytes 20971520 | tf_op jit(solution)/shard_map/okij,okjm->oim/dot_general | solution.py:41
  41.7 1.5 copy-done
  43.2 0.6 convert_reduce_fusion
  43.9 41.4 %reduce-scatter.2.cloned.1.call-done = f32[8,128,128]{1,2,0:T(8,128)} async-done(((f32[64,128,128]{1,2,0:T(8,128)}), f32[8,128,128]{1,2,0:T(8,128)}) %reduce-scatter.2.cloned.1.call-update) | async-done | bytes 524304 | tf_op jit(solution)/shard_map/reduce_scatter | solution.py:40
  85.3 1.1 reduce_sum.19
  86.4 0.1 subtract_multiply_fusion.3
  86.5 2.5 convolution_bitcast_fusion
  89.0 1.6 convolution_bitcast_fusion.3
  90.5 79.5 %psum.15 = f32[128]{0:T(128)S(1)} all-reduce(f32[128]{0:T(128)S(1)} %convolution_bitcast_fusion.3), channel_id=1, replica_groups=mesh['tile'=32,'lev'=8] {'tile','lev'}, use_global_device_ids=true, to_apply=%region_6.7 | all-reduce | flops 128 | bytes 1024 | tf_op jit(solution)/shard_map/psum | solution.py:54
  170.0 161.5 %all-reduce.2.cloned.1.call-done = f32[128,128]{1,0:T(8,128)} async-done(((f32[128,128]{1,0:T(8,128)}), f32[128,128]{1,0:T(8,128)}) %all-reduce.2.cloned.1.call-update) | async-done | bytes 65552 | tf_op jit(solution)/shard_map/psum | solution.py:54
  331.5 0.9 convert_add_fusion
  332.3 0.1 copy.17
  332.4 0.9 fusion.17
  333.3 11.7 %cholesky.18 = f32[128,128]{1,0:T(8,128)S(1)} custom-call(f32[128,128]{1,0:T(8,128)S(1)} %fusion.17), custom_call_target="Cholesky" | custom-call | tf_op jit(solution)/shard_map/jit(cholesky)/cholesky | solution.py:55
  345.0 0.6 compare_reduce_fusion
  345.7 0.7 fusion.13
  346.3 9.8 %custom-call.6 = f32[1,128,128]{1,2,0:T(8,128)S(1)} custom-call(f32[1,128,128]{2,1,0:T(8,128)S(1)} %fusion.13), custom_call_target="InvertDiagBlocksLowerTriangular" | custom-call | tf_op jit(solution)/shard_map/triangular_solve | solution.py:56
  356.1 0.2 fusion.15
  356.4 0.2 convolution_bitcast_fusion.2
  356.6 0.2 fusion.8
  356.8 0.7 copy.19
  357.5 5.3 %add_convert_fusion = bf16[4,2048,128]{2,1,0:T(8,128)(2,1)} fusion(bf16[4,2048,128]{2,1,0:T(8,128)(2,1)S(1)} %copy-done, f32[4,2048]{1,0:T(4,128)S(1)} %broadcast_multiply_fusion, f32[128,128]{0,1:T(8,128)S(1)} %bitcast_add_fusion), kind=kOutput, calls=%fused_computation.6 | convolution fusion | flops 273694720 | bytes 4292608 | tf_op jit(solution)/shard_map/dot_general | solution.py:62
  (15 shorter events, 0.2 us)
Async XLA Ops:
  7.2 78.2 %reduce-scatter.2.cloned.1.call-start = ((), (), s32[]{:S(2)}) async-start(), calls=%async_computation.1 | async-start | bytes 4718592 | tf_op jit(solution)/shard_map/reduce_scatter | solution.py:40
  8.3 9.0 %collective-permute-start = (bf16[4,256,128]{2,1,0:T(8,128)(2,1)S(1)}, bf16[4,256,128]{2,1,0:T(8,128)(2,1)S(1)}, u32[]{:S(2)}, u32[]{:S(2)}) collective-permute-start(bf16[4,256,128]{2,1,0:T(8,128)(2,1)S(1)} %get-tuple-element.6), channel_id=1, source_target_pairs={{0,8},{8,16},{16,24},{24,32},{32,40},{40,48},{48,56},{56,64},{64,7... | collective-permute-start | bytes 786440 | tf_op jit(solution)/shard_map/ppermute | solution.py:17
  12.3 8.8 %collective-permute-start.1 = (bf16[4,256,128]{2,1,0:T(8,128)(2,1)S(1)}, bf16[4,256,128]{2,1,0:T(8,128)(2,1)S(1)}, u32[]{:S(2)}, u32[]{:S(2)}) collective-permute-start(bf16[4,256,128]{2,1,0:T(8,128)(2,1)S(1)} %get-tuple-element.7), channel_id=1, source_target_pairs={{8,0},{16,8},{24,16},{32,24},{40,32},{48,40},{56,48},{64,56},{72,6... | collective-permute-start | bytes 786440 | tf_op jit(solution)/shard_map/ppermute | solution.py:18
  41.6 1.6 copy-start
  41.6 44.8 %copy-start.1 = (f32[8,128]{1,0:T(8,128)S(1)}, f32[8,128]{1,0:T(8,128)}, u32[]{:S(2)}) copy-start(f32[8,128]{1,0:T(8,128)} %param.12) | copy-start | bytes 12292
  41.6 44.8 %copy-start.2 = (f32[8,128]{1,0:T(8,128)S(1)}, f32[8,128]{1,0:T(8,128)}, u32[]{:S(2)}) copy-start(f32[8,128]{1,0:T(8,128)} %param.13) | copy-start | bytes 12292
  41.6 44.8 %copy-start.3 = (s32[8]{0:T(128)S(1)}, s32[8]{0:T(128)}, u32[]{:S(2)}) copy-start(s32[8]{0:T(128)} %param.11) | copy-start | bytes 100
  41.7 289.8 %all-reduce.2.cloned.1.call-start = ((), (), s32[]{:S(2)}) async-start(), calls=%async_computation.2 | async-start | bytes 131072 | tf_op jit(solution)/shard_map/psum | solution.py:54
Sparse Core Ops, SparseCore 0:
  41.8 43.4 reduce-scatter.1
  91.4 240.0 all-reduce.1
where the time goes:
time: 370 us
  waiting for transfers between devices  209 us (56%)
  blocking collectives  79.5 us (21%)
  other arithmetic  28.9 us (8%)
  matrix products  20 us (5%)
  between operations  14.2 us (4%)
  local copies, waits for them, and re-layouts  12.2 us (3%)
  starting transfers between devices  5.42 us (1%)
    psum x1, waiting for transfers between devices, shards(): gram, pull = lax.psum((gram_local, pull_local), ('tile', 'lev'))  161 us
    psum x1, blocking collectives, shards(): gram, pull = lax.psum((gram_local, pull_local), ('tile', 'lev'))  79.5 us
    reduce_scatter x1, waiting for transfers between devices, shards(): lax.psum_scatter(jnp.einsum('okij,okjm->oim', operator_blocks, chosen, pr...  41.4 us
    another operation x3, other arithmetic, shards(): lower = jnp.linalg.cholesky(identity + gram)  12.4 us
    another operation x2, other arithmetic, shards(): lax.linalg.triangular_solve(lower, identity, left_side=True, lower=True)  10.5 us
    dot_general x1, matrix products, shards(): jnp.einsum('okij,okjm->oim', operator_blocks, chosen, preferred_element_t...  10.1 us
    gather x1, local copies, waits for them, and re-layouts, shards(): chosen = column_blocks[flat_index]  8.62 us
  transfers between devices with their start and end apart: 4, of which 4 were waited for; matrix products, arithmetic and copies ran while one was open for 1% of the time, Pallas kernels for 0%

commit v1 on v0

--- a/solution.py
+++ b/solution.py
@@ -51,7 +51,7 @@
     gram_local = jnp.dot(spread.T, spread, precision=highest, preferred_element_type=jnp.float32)
     pull_local = jnp.dot(innovation, spread, precision=highest, preferred_element_type=jnp.float32)
     identity = jnp.eye(ensemble, dtype=jnp.float32)
-    gram, pull = lax.psum((gram_local, pull_local), ("tile", "lev"))
+    gram, pull = lax.psum(lax.psum((gram_local, pull_local), "lev"), "tile")
     lower = jnp.linalg.cholesky(identity + gram)
     inverse = lax.linalg.triangular_solve(lower, identity, left_side=True, lower=True)
     shift_weights = jnp.dot(inverse.T, jnp.dot(inverse, pull, precision=highest), precision=highest)

time: 370 us -> 334 us (0.903)
  waiting for transfers between devices: 209 us -> 174 us
  blocking collectives: 79.5 us -> 75.6 us
    psum x1 -> x2, waiting for transfers between devices: 161 us -> 126 us  [shards(): gram, pull = lax.psum(lax.psum((gram_local, pull_local), 'lev'), 'tile')]
    psum x1 -> x2, blocking collectives: 79.5 us -> 75.6 us  [shards(): gram, pull = lax.psum(lax.psum((gram_local, pull_local), 'lev'), 'tile')]
  transfers between devices with their start and end apart: 4 -> 5, of which waited for: 4 -> 5; matrix products, arithmetic and copies ran while one was open for 1% -> 1% of each run, Pallas kernels for 0% -> 0%
where the time goes in v1:
time: 334 us; the launch traced here: 331 us
  waiting for transfers between devices  174 us (52%)
  blocking collectives  75.6 us (23%)
  other arithmetic  28.9 us (9%)
  matrix products  20 us (6%)
  between operations  13.9 us (4%)
  local copies, waits for them, and re-layouts  12.2 us (4%)
  starting transfers between devices  5.46 us (2%)
    psum x2, waiting for transfers between devices, shards(): gram, pull = lax.psum(lax.psum((gram_local, pull_local), 'lev'), 'tile')  126 us
    psum x2, blocking collectives, shards(): gram, pull = lax.psum(lax.psum((gram_local, pull_local), 'lev'), 'tile')  75.6 us
    reduce_scatter x1, waiting for transfers between devices, shards(): lax.psum_scatter(jnp.einsum('okij,okjm->oim', operator_blocks, chosen, pr...  41.5 us
    another operation x3, other arithmetic, shards(): lower = jnp.linalg.cholesky(identity + gram)  12.4 us
    another operation x2, other arithmetic, shards(): lax.linalg.triangular_solve(lower, identity, left_side=True, lower=True)  10.5 us
    dot_general x1, matrix products, shards(): jnp.einsum('okij,okjm->oim', operator_blocks, chosen, preferred_element_t...  10.1 us
    gather x1, local copies, waits for them, and re-layouts, shards(): chosen = column_blocks[flat_index]  8.62 us
  transfers between devices with their start and end apart: 5, of which 5 were waited for; matrix products, arithmetic and copies ran while one was open for 1% of the time, Pallas kernels for 0%

profile of v1, /device:TPU:1, one launch (start us, length us, event | category | flops | bytes accessed | tf_op | source)
XLA Modules:
  0.0 330.6 jit_solution(8091747654081412660)
XLA Ops:
  7.2 1.1 fusion.23
  8.3 4.0 %collective-permute-start = (bf16[4,256,128]{2,1,0:T(8,128)(2,1)S(1)}, bf16[4,256,128]{2,1,0:T(8,128)(2,1)S(1)}, u32[]{:S(2)}, u32[]{:S(2)}) collective-permute-start(bf16[4,256,128]{2,1,0:T(8,128)(2,1)S(1)} %get-tuple-element.6), channel_id=1, source_target_pairs={{0,8},{8,16},{16,24},{24,32},{32,40},{40,48},{48,56},{56,64},{64,7... | collective-permute-start | bytes 786440 | tf_op jit(solution)/shard_map/ppermute | solution.py:17
  12.3 1.3 collective-permute-start.1
  13.6 0.7 compare_select_fusion
  14.3 0.1 copy.14
  14.4 0.1 reshape.63
  14.6 2.7 collective-permute-done
  17.3 3.8 %collective-permute-done.1 = bf16[4,256,128]{2,1,0:T(8,128)(2,1)S(1)} collective-permute-done((bf16[4,256,128]{2,1,0:T(8,128)(2,1)S(1)}, bf16[4,256,128]{2,1,0:T(8,128)(2,1)S(1)}, u32[]{:S(2)}, u32[]{:S(2)}) %collective-permute-start.1) | collective-permute-done | bytes 262176 | tf_op jit(solution)/shard_map/ppermute | solution.py:18
  21.1 1.8 pad_maximum_fusion
  22.9 8.6 %gather_fusion = bf16[256,128,128]{2,1,0:T(8,128)(2,1)} fusion(bf16[80,128,128]{2,1,0:T(8,128)(2,1)S(1)} %bitcast.54, s32[1024]{0:T(1024)S(1)} %pad_clamp_fusion), kind=kCustom, calls=%fused_computation | custom fusion | bytes 16778240 | tf_op jit(solution)/shard_map/gather | solution.py:39
  31.5 10.1 %fusion.3 = f32[64,128,128]{1,2,0:T(8,128)} fusion(bf16[64,4,128,128]{3,2,1,0:T(8,128)(2,1)} %bitcast.55, bf16[1,64,4,128,128]{4,3,2,1,0:T(8,128)(2,1)} %param.8), kind=kOutput, calls=%fused_computation.8 | convolution fusion | flops 1073741824 | bytes 20971520 | tf_op jit(solution)/shard_map/okij,okjm->oim/dot_general | solution.py:41
  41.7 1.5 copy-done
  43.2 0.6 convert_reduce_fusion
  43.9 41.5 %reduce-scatter.2.cloned.1.call-done = f32[8,128,128]{1,2,0:T(8,128)} async-done(((f32[64,128,128]{1,2,0:T(8,128)}), f32[8,128,128]{1,2,0:T(8,128)}) %reduce-scatter.2.cloned.1.call-update) | async-done | bytes 524304 | tf_op jit(solution)/shard_map/reduce_scatter | solution.py:40
  85.3 1.1 reduce_sum.19
  86.5 2.5 convolution_bitcast_fusion
  89.1 63.7 %all-reduce.3.cloned.1.call-done = f32[128,128]{1,0:T(8,128)} async-done(((f32[128,128]{1,0:T(8,128)}), f32[128,128]{1,0:T(8,128)}) %all-reduce.3.cloned.1.call-update) | async-done | bytes 65552 | tf_op jit(solution)/shard_map/psum | solution.py:54
  152.8 1.6 convolution_bitcast_fusion.3
  154.3 14.5 %psum.30 = f32[128]{0:T(128)S(1)} all-reduce(f32[128]{0:T(128)S(1)} %convolution_bitcast_fusion.3), channel_id=1, replica_groups=mesh['tile'=32,'lev'=8] {'lev'}, use_global_device_ids=true, to_apply=%region_7.8 | all-reduce | flops 128 | bytes 1024 | tf_op jit(solution)/shard_map/psum | solution.py:54
  168.8 61.1 %psum.31 = f32[128]{0:T(128)S(1)} all-reduce(f32[128]{0:T(128)S(1)} %psum.30), channel_id=1, replica_groups=mesh['tile'=32,'lev'=8] {'tile'}, use_global_device_ids=true, to_apply=%region_8.9 | all-reduce | flops 128 | bytes 1024 | tf_op jit(solution)/shard_map/psum | solution.py:54
  229.9 62.8 %all-reduce.5.cloned.1.call-done = f32[128,128]{1,0:T(8,128)} async-done(((f32[128,128]{1,0:T(8,128)}), f32[128,128]{1,0:T(8,128)}) %all-reduce.5.cloned.1.call-update) | async-done | bytes 65552 | tf_op jit(solution)/shard_map/psum | solution.py:54
  292.7 0.9 convert_add_fusion
  293.6 0.9 fusion.17
  294.5 11.7 %cholesky.18 = f32[128,128]{1,0:T(8,128)S(1)} custom-call(f32[128,128]{1,0:T(8,128)S(1)} %fusion.17), custom_call_target="Cholesky" | custom-call | tf_op jit(solution)/shard_map/jit(cholesky)/cholesky | solution.py:55
  306.3 0.6 compare_reduce_fusion
  306.9 0.7 fusion.13
  307.6 9.8 %custom-call.6 = f32[1,128,128]{1,2,0:T(8,128)S(1)} custom-call(f32[1,128,128]{2,1,0:T(8,128)S(1)} %fusion.13), custom_call_target="InvertDiagBlocksLowerTriangular" | custom-call | tf_op jit(solution)/shard_map/triangular_solve | solution.py:56
  317.4 0.2 fusion.15
  317.6 0.2 convolution_bitcast_fusion.2
  317.8 0.2 fusion.8
  318.0 0.7 copy.19
  318.8 5.3 %add_convert_fusion = bf16[4,2048,128]{2,1,0:T(8,128)(2,1)} fusion(bf16[4,2048,128]{2,1,0:T(8,128)(2,1)S(1)} %copy-done, f32[4,2048]{1,0:T(4,128)S(1)} %broadcast_multiply_fusion, f32[128,128]{0,1:T(8,128)S(1)} %bitcast_add_fusion), kind=kOutput, calls=%fused_computation.6 | convolution fusion | flops 273694720 | bytes 4292608 | tf_op jit(solution)/shard_map/dot_general | solution.py:62
  (19 shorter events, 0.4 us)
Async XLA Ops:
  7.2 78.2 %reduce-scatter.2.cloned.1.call-start = ((), (), s32[]{:S(2)}) async-start(), calls=%async_computation.1 | async-start | bytes 4718592 | tf_op jit(solution)/shard_map/reduce_scatter | solution.py:40
  8.3 9.0 %collective-permute-start = (bf16[4,256,128]{2,1,0:T(8,128)(2,1)S(1)}, bf16[4,256,128]{2,1,0:T(8,128)(2,1)S(1)}, u32[]{:S(2)}, u32[]{:S(2)}) collective-permute-start(bf16[4,256,128]{2,1,0:T(8,128)(2,1)S(1)} %get-tuple-element.6), channel_id=1, source_target_pairs={{0,8},{8,16},{16,24},{24,32},{32,40},{40,48},{48,56},{56,64},{64,7... | collective-permute-start | bytes 786440 | tf_op jit(solution)/shard_map/ppermute | solution.py:17
  12.3 8.8 %collective-permute-start.1 = (bf16[4,256,128]{2,1,0:T(8,128)(2,1)S(1)}, bf16[4,256,128]{2,1,0:T(8,128)(2,1)S(1)}, u32[]{:S(2)}, u32[]{:S(2)}) collective-permute-start(bf16[4,256,128]{2,1,0:T(8,128)(2,1)S(1)} %get-tuple-element.7), channel_id=1, source_target_pairs={{8,0},{16,8},{24,16},{32,24},{40,32},{48,40},{56,48},{64,56},{72,6... | collective-permute-start | bytes 786440 | tf_op jit(solution)/shard_map/ppermute | solution.py:18
  41.6 1.6 copy-start
  41.6 44.8 %copy-start.1 = (f32[8,128]{1,0:T(8,128)S(1)}, f32[8,128]{1,0:T(8,128)}, u32[]{:S(2)}) copy-start(f32[8,128]{1,0:T(8,128)} %param.12) | copy-start | bytes 12292
  41.6 44.8 %copy-start.2 = (f32[8,128]{1,0:T(8,128)S(1)}, f32[8,128]{1,0:T(8,128)}, u32[]{:S(2)}) copy-start(f32[8,128]{1,0:T(8,128)} %param.13) | copy-start | bytes 12292
  41.6 44.8 %copy-start.3 = (s32[8]{0:T(128)S(1)}, s32[8]{0:T(128)}, u32[]{:S(2)}) copy-start(s32[8]{0:T(128)} %param.11) | copy-start | bytes 100
  41.7 111.1 %all-reduce.3.cloned.1.call-start = ((), (), s32[]{:S(2)}) async-start(), calls=%async_computation.2 | async-start | bytes 131072 | tf_op jit(solution)/shard_map/psum | solution.py:54
  89.0 203.7 %all-reduce.5.cloned.1.call-start = ((), (), s32[]{:S(2)}) async-start(), calls=%async_computation.3 | async-start | bytes 131072 | tf_op jit(solution)/shard_map/psum | solution.py:54
Sparse Core Ops, SparseCore 0:
  41.8 43.4 reduce-scatter.1
  89.1 63.5 all-reduce.2
  156.6 136.0 all-reduce.4
